TPU v7x, 32 devices: a whole 2x2x4 slice. The times are simulated.
32 devices in a mesh: groups: 2 (over y), dp: 4 (over x, core), tensor: 4 (over z).
Axes of the slice: x: 2, y: 2, z: 4, core: 2. Of those that a mesh axis runs over, the one named last changes fastest.
Arguments:
- query_inputs: bfloat16 [4096, 5120], P('dp', 'tensor'), may hold values from -6 to 6
- query_grads: bfloat16 [4096, 13824], P('dp', 'tensor'), may hold values from -1.09375 to 1.09375
- input_factor: bfloat16 [64, 5120], P(None, 'tensor'), may hold values from -0.078125 to 0.078125
- output_factor: bfloat16 [64, 13824], P(None, 'tensor'), may hold values from -0.0546875 to 0.0546875
- train_store: bfloat16 [8192, 4096], P(('groups', 'dp', 'tensor')), parts along dimension 0, may hold values from -0.09375 to 0.09375
Outputs:
- scores: float32 [8192, 128], P(('groups', 'dp', 'tensor')), parts along dimension 0
There are 2 independent parts, one for each index of `groups`. A program takes and returns all parts, laid end to end along the dimension named above; an argument that names none is the same for every part. Nothing has to cross between parts.
All inputs are finite; a program needn't handle non-finite values.
Results may differ from a plain program's by a relative error of at most 0.0029.
Values may be sent and summed in bfloat16 or wider, within the bound.
A program may use at most 64 MiB of HBM per device.

v0:
```python
import jax
import jax.numpy as jnp
from jax import lax
from jax.sharding import PartitionSpec as P

K = 64
SEQ = 32


def from_behind(value, axis, steps):
    count = lax.axis_size(axis)
    pairs = [(source, (source + steps) % count) for source in range(count)]
    return lax.ppermute(value, axis, pairs)


def outer_blocks(inputs_rows, grads_rows):
    examples = inputs_rows.shape[0] // SEQ
    blocks = jnp.einsum(
        "eto,eti->eoi",
        grads_rows.reshape(examples, SEQ, K),
        inputs_rows.reshape(examples, SEQ, K),
        precision=lax.Precision.HIGHEST,
    )
    return blocks.reshape(examples, K * K).astype(jnp.bfloat16)


def local(query_inputs, query_grads, input_factor, output_factor, train_store):
    inputs_part = jnp.einsum(
        "td,kd->tk", query_inputs, input_factor, preferred_element_type=jnp.float32
    )
    grads_part = jnp.einsum(
        "tf,kf->tk", query_grads, output_factor, preferred_element_type=jnp.float32
    )
    inputs_full, grads_full = lax.psum((inputs_part, grads_part), "tensor")
    block = outer_blocks(inputs_full, grads_full)

    def score_piece(piece):
        return lax.dot_general(
            train_store, piece, (((1,), (1,)), ((), ())), preferred_element_type=jnp.float32
        )

    def place_block(scores, piece, start):
        scored = score_piece(piece)
        return lax.dynamic_update_slice_in_dim(scores, scored, start, 1)

    per_owner = block.shape[0]
    cycle_size = lax.axis_size("dp")
    own_index = lax.axis_index("dp")
    all_queries = per_owner * cycle_size
    scores_empty = jnp.zeros((train_store.shape[0], all_queries), jnp.float32)
    scores = place_block(scores_empty, block, own_index * per_owner)

    def cycle_step(turn, carry):
        held, scores = carry
        held = from_behind(held, "dp", 1)
        owner = (own_index - turn) % cycle_size
        return (held, place_block(scores, held, owner * per_owner))

    held, scores = lax.fori_loop(1, cycle_size, cycle_step, (block, scores))
    return scores


def solution(mesh):
    return jax.shard_map(
        local,
        mesh=mesh,
        in_specs=(
            P("dp", "tensor"),
            P("dp", "tensor"),
            P(None, "tensor"),
            P(None, "tensor"),
            P(("groups", "dp", "tensor"), None),
        ),
        out_specs=P(("groups", "dp", "tensor"), None),
        check_vma=False,
    )
```

profile of v0, /device:TPU:1, one launch (start us, length us, event | category | flops | bytes accessed | tf_op | source)
XLA Modules:
  0.0 106.0 jit_solution(8590677945648474546)
XLA Ops:
  6.5 0.0 copy-start
  6.5 0.0 copy-start.1
  6.5 0.0 all-reduce.3.cloned.1.call-start
  6.5 5.9 %fusion.1 = f32[1024,64]{1,0:T(8,128)} fusion(bf16[1024,3456]{1,0:T(8,128)(2,1)} %param.8, bf16[64,3456]{1,0:T(8,128)(2,1)} %param.10), kind=kOutput, calls=%fused_computation.4 | convolution fusion | flops 452984832 | bytes 7782400 | tf_op jit(solution)/shard_map/tf,kf->tk/dot_general | solution.py:31
  12.5 0.0 copy-done
  12.5 0.0 copy-done.1
  12.5 1.6 %fusion.2 = f32[1024,64]{1,0:T(8,128)} fusion(bf16[1024,1280]{1,0:T(8,128)(2,1)S(1)} %copy-done, bf16[64,1280]{1,0:T(8,128)(2,1)S(1)} %copy-done.1), kind=kOutput, calls=%fused_computation.5 | convolution fusion | flops 167772160 | bytes 3047424 | tf_op jit(solution)/shard_map/td,kd->tk/dot_general | solution.py:28
  14.1 0.0 all-reduce.3.cloned.1.call-update
  14.2 54.6 %all-reduce.3.cloned.1.call-done = (f32[32,32,64]{2,1,0:T(8,128)}, f32[32,32,64]{2,1,0:T(8,128)}) async-done(((f32[32,32,64]{2,1,0:T(8,128)}, f32[32,32,64]{2,1,0:T(8,128)}), (f32[32,32,64]{2,1,0:T(8,128)}, f32[32,32,64]{2,1,0:T(8,128)})) %all-reduce.3.cloned.1.call-update) | async-done | bytes 524304 | tf_op jit(solution)/shard_map/psum | solution.py:34
  68.8 3.1 %convolution_convert_fusion = bf16[32,64,64]{2,1,0:T(8,128)(2,1)S(1)} fusion(f32[32,32,64]{2,1,0:T(8,128)} %get-tuple-element.149, f32[32,32,64]{2,1,0:T(8,128)} %get-tuple-element.150), kind=kOutput, calls=%fused_computation.1 | convolution fusion | flops 50462720 | bytes 786432 | tf_op jit(solution)/shard_map/eto,eti->eoi/dot_general | solution.py:18
  71.9 0.5 convert_element_type.7
  72.4 2.3 %fusion = f32[256,128]{0,1:T(8,128)S(1)} fusion(f32[256,128]{0,1:T(8,128)S(1)} %broadcast_in_dim.3, s32[]{:T(128)S(6)} %select_n.33, bf16[32,4096]{1,0:T(8,128)(2,1)S(1)} %convert_element_type.7, bf16[256,4096]{1,0:T(8,128)(2,1)} %param.11), kind=kOutput, calls=%fused_computation.3 | convolution fusion | flops 67108864 | bytes 2392068 | tf_op jit(solution)/shard_map/dot_general | solution.py:38
  74.7 23.7 %while.17 = (s32[]{:T(128)}, bf16[32,4096]{1,0:T(8,128)(2,1)S(1)}, f32[256,128]{0,1:T(8,128)S(1)}, bf16[256,4096]{1,0:T(8,128)(2,1)}, s32[]{:T(128)}, /*index=5*...) while((s32[]{:T(128)}, bf16[32,4096]{1,0:T(8,128)(2,1)S(1)}, ...), condition=%wide.region_3.4_spmd, body=%wide.region_2.3_spmd.sunk | while | flops 67108880 | bytes 3965248 | solution.py:59
  74.7 1.6 %collective-permute-start = (bf16[32,4096]{1,0:T(8,128)(2,1)S(1)}, bf16[32,4096]{1,0:T(8,128)(2,1)S(1)}, u32[]{:S(2)}, u32[]{:S(2)}) collective-permute-start(bf16[32,4096]{1,0:T(8,128)(2,1)S(1)} %get-tuple-element.194), channel_id=1, source_target_pairs={{0,4},{4,8},{8,12},{12,0},{1,5},{5,9},{9,13},{13,1},{2,6},{6,10},{... | collective-permute-start | bytes 786440 | tf_op jit(solution)/shard_map/while/body/eval_jaxpr/ppermute | solution.py:13
  76.3 3.3 %collective-permute-done = bf16[32,4096]{1,0:T(8,128)(2,1)S(1)} collective-permute-done((bf16[32,4096]{1,0:T(8,128)(2,1)S(1)}, bf16[32,4096]{1,0:T(8,128)(2,1)S(1)}, u32[]{:S(2)}, u32[]{:S(2)}) %collective-permute-start) | collective-permute-done | bytes 262176 | tf_op jit(solution)/shard_map/while/body/eval_jaxpr/ppermute | solution.py:13
  79.7 2.3 %convolution_dynamic-update-slice_fusion.2 = f32[256,128]{0,1:T(8,128)S(1)} fusion(f32[256,128]{0,1:T(8,128)S(1)} %get-tuple-element.195, s32[]{:T(128)S(6)} %select_n.37, bf16[256,4096]{1,0:T(8,128)(2,1)} %get-tuple-element.207, bf16[32,4096]{1,0:T(8,128)(2,1)S(1)} %collective-permute-done), kind=kOutput, calls=%fused_computation.clone.1 | convolution fusion | flops 67108864 | bytes 2392068 | tf_op jit(solution)/shard_map/while/body/eval_jaxpr/dot_general | solution.py:38
  82.0 2.5 %collective-permute-start = (bf16[32,4096]{1,0:T(8,128)(2,1)S(1)}, bf16[32,4096]{1,0:T(8,128)(2,1)S(1)}, u32[]{:S(2)}, u32[]{:S(2)}) collective-permute-start(bf16[32,4096]{1,0:T(8,128)(2,1)S(1)} %get-tuple-element.194), channel_id=1, source_target_pairs={{0,4},{4,8},{8,12},{12,0},{1,5},{5,9},{9,13},{13,1},{2,6},{6,10},{... | collective-permute-start | bytes 786440 | tf_op jit(solution)/shard_map/while/body/eval_jaxpr/ppermute | solution.py:13
  84.5 3.3 %collective-permute-done = bf16[32,4096]{1,0:T(8,128)(2,1)S(1)} collective-permute-done((bf16[32,4096]{1,0:T(8,128)(2,1)S(1)}, bf16[32,4096]{1,0:T(8,128)(2,1)S(1)}, u32[]{:S(2)}, u32[]{:S(2)}) %collective-permute-start) | collective-permute-done | bytes 262176 | tf_op jit(solution)/shard_map/while/body/eval_jaxpr/ppermute | solution.py:13
  87.9 2.3 %convolution_dynamic-update-slice_fusion.2 = f32[256,128]{0,1:T(8,128)S(1)} fusion(f32[256,128]{0,1:T(8,128)S(1)} %get-tuple-element.195, s32[]{:T(128)S(6)} %select_n.37, bf16[256,4096]{1,0:T(8,128)(2,1)} %get-tuple-element.207, bf16[32,4096]{1,0:T(8,128)(2,1)S(1)} %collective-permute-done), kind=kOutput, calls=%fused_computation.clone.1 | convolution fusion | flops 67108864 | bytes 2392068 | tf_op jit(solution)/shard_map/while/body/eval_jaxpr/dot_general | solution.py:38
  90.2 2.5 %collective-permute-start = (bf16[32,4096]{1,0:T(8,128)(2,1)S(1)}, bf16[32,4096]{1,0:T(8,128)(2,1)S(1)}, u32[]{:S(2)}, u32[]{:S(2)}) collective-permute-start(bf16[32,4096]{1,0:T(8,128)(2,1)S(1)} %get-tuple-element.194), channel_id=1, source_target_pairs={{0,4},{4,8},{8,12},{12,0},{1,5},{5,9},{9,13},{13,1},{2,6},{6,10},{... | collective-permute-start | bytes 786440 | tf_op jit(solution)/shard_map/while/body/eval_jaxpr/ppermute | solution.py:13
  92.7 3.3 %collective-permute-done = bf16[32,4096]{1,0:T(8,128)(2,1)S(1)} collective-permute-done((bf16[32,4096]{1,0:T(8,128)(2,1)S(1)}, bf16[32,4096]{1,0:T(8,128)(2,1)S(1)}, u32[]{:S(2)}, u32[]{:S(2)}) %collective-permute-start) | collective-permute-done | bytes 262176 | tf_op jit(solution)/shard_map/while/body/eval_jaxpr/ppermute | solution.py:13
  96.1 2.3 %convolution_dynamic-update-slice_fusion.2 = f32[256,128]{0,1:T(8,128)S(1)} fusion(f32[256,128]{0,1:T(8,128)S(1)} %get-tuple-element.195, s32[]{:T(128)S(6)} %select_n.37, bf16[256,4096]{1,0:T(8,128)(2,1)} %get-tuple-element.207, bf16[32,4096]{1,0:T(8,128)(2,1)S(1)} %collective-permute-done), kind=kOutput, calls=%fused_computation.clone.1 | convolution fusion | flops 67108864 | bytes 2392068 | tf_op jit(solution)/shard_map/while/body/eval_jaxpr/dot_general | solution.py:38
  98.4 0.8 copy.11
  (4 shorter events, 0.1 us)
Async XLA Ops:
  6.5 6.0 %copy-start = (bf16[1024,1280]{1,0:T(8,128)(2,1)S(1)}, bf16[1024,1280]{1,0:T(8,128)(2,1)}, u32[]{:S(2)}) copy-start(bf16[1024,1280]{1,0:T(8,128)(2,1)} %param.7) | copy-start | bytes 7864324
  6.5 6.0 %copy-start.1 = (bf16[64,1280]{1,0:T(8,128)(2,1)S(1)}, bf16[64,1280]{1,0:T(8,128)(2,1)}, u32[]{:S(2)}) copy-start(bf16[64,1280]{1,0:T(8,128)(2,1)} %param.9) | copy-start | bytes 491524
  6.5 62.2 %all-reduce.3.cloned.1.call-start = ((), (), s32[]{:S(2)}) async-start(), calls=%async_computation | async-start | bytes 2097152 | tf_op jit(solution)/shard_map/psum | solution.py:34
  74.7 4.9 %collective-permute-start = (bf16[32,4096]{1,0:T(8,128)(2,1)S(1)}, bf16[32,4096]{1,0:T(8,128)(2,1)S(1)}, u32[]{:S(2)}, u32[]{:S(2)}) collective-permute-start(bf16[32,4096]{1,0:T(8,128)(2,1)S(1)} %get-tuple-element.194), channel_id=1, source_target_pairs={{0,4},{4,8},{8,12},{12,0},{1,5},{5,9},{9,13},{13,1},{2,6},{6,10},{... | collective-permute-start | bytes 786440 | tf_op jit(solution)/shard_map/while/body/eval_jaxpr/ppermute | solution.py:13
  82.0 5.8 %collective-permute-start = (bf16[32,4096]{1,0:T(8,128)(2,1)S(1)}, bf16[32,4096]{1,0:T(8,128)(2,1)S(1)}, u32[]{:S(2)}, u32[]{:S(2)}) collective-permute-start(bf16[32,4096]{1,0:T(8,128)(2,1)S(1)} %get-tuple-element.194), channel_id=1, source_target_pairs={{0,4},{4,8},{8,12},{12,0},{1,5},{5,9},{9,13},{13,1},{2,6},{6,10},{... | collective-permute-start | bytes 786440 | tf_op jit(solution)/shard_map/while/body/eval_jaxpr/ppermute | solution.py:13
  90.2 5.8 %collective-permute-start = (bf16[32,4096]{1,0:T(8,128)(2,1)S(1)}, bf16[32,4096]{1,0:T(8,128)(2,1)S(1)}, u32[]{:S(2)}, u32[]{:S(2)}) collective-permute-start(bf16[32,4096]{1,0:T(8,128)(2,1)S(1)} %get-tuple-element.194), channel_id=1, source_target_pairs={{0,4},{4,8},{8,12},{12,0},{1,5},{5,9},{9,13},{13,1},{2,6},{6,10},{... | collective-permute-start | bytes 786440 | tf_op jit(solution)/shard_map/while/body/eval_jaxpr/ppermute | solution.py:13
Sparse Core Ops, SparseCore 0:
  14.3 54.4 all-reduce.2
where the time goes:
time: 108 us; the launch traced here: 106 us
  waiting for transfers between devices  64.6 us (60%)
  matrix products  20 us (19%)
  between operations  13.4 us (12%)
  starting transfers between devices  6.66 us (6%)
  local copies, waits for them, and re-layouts  1.29 us (1%)
    psum x1, waiting for transfers between devices, local(): inputs_full, grads_full = lax.psum((inputs_part, grads_part), 'tensor')  54.6 us
    ppermute x3, waiting for transfers between devices, from_behind(): return lax.ppermute(value, axis, pairs)  9.95 us
    dot_general x4, matrix products, score_piece(): lax.dot_general(train_store, piece, (((1,), (1,)), ((), ())), preferred_e...  9.27 us
    ppermute x3, starting transfers between devices, from_behind(): return lax.ppermute(value, axis, pairs)  6.66 us
    dot_general x1, matrix products, local(): jnp.einsum('tf,kf->tk', query_grads, output_factor, preferred_element_typ...  5.95 us
    dot_general x1, matrix products, outer_blocks(): jnp.einsum('eto,eti->eoi', grads_rows.reshape(examples, SEQ, K), inputs_r...  3.15 us
  transfers between devices with their start and end apart: 4, of which 4 were waited for; matrix products, arithmetic and copies ran while one was open for 0% of the time, Pallas kernels for 0%

commit v1 on v0

v1 whole, which is shorter than its diff:
```python
import jax
import jax.numpy as jnp
from jax import lax
from jax.experimental import pallas as pl
from jax.experimental.pallas import tpu as pltpu
from jax.sharding import PartitionSpec as P

K = 64
SEQ = 32
HIGHEST = lax.Precision.HIGHEST


def dot_rows(a, b):
    return lax.dot_general(a, b, (((1,), (1,)), ((), ())), preferred_element_type=jnp.float32)


def fused_kernel(
    qi_hbm, qg_hbm, fi_hbm, fo_hbm, store_hbm, out_ref,
    qi, qg, fi, fo, store, part, got, turned, spread, blocks, wide,
    load_sem, rs_send, rs_recv, ag_send, ag_recv,
):
    depth = lax.axis_size("tensor")
    rows = qi.shape[1]
    y = lax.axis_index("groups")
    dp = lax.axis_index("dp")
    z = lax.axis_index("tensor")
    x = dp // 2
    core = dp % 2
    other_core = {"dp": x * 2 + (1 - core)}
    other_x = {"dp": (1 - x) * 2 + core}
    other_y = {"groups": 1 - y}
    order = (2, 1, 3, 0)

    def load(source, target, index):
        return pltpu.make_async_copy(source, target, load_sem.at[index])

    def chunk_loads(step):
        target = lax.rem(z + step, depth)
        start = pl.multiple_of((y * depth + target) * rows, rows)
        return (
            load(qi_hbm.at[pl.ds(start, rows), :], qi.at[step], 3 + 2 * step),
            load(qg_hbm.at[pl.ds(start, rows), :], qg.at[step], 4 + 2 * step),
        )

    load(fi_hbm, fi, 0).start()
    load(fo_hbm, fo, 1).start()
    for step in order:
        for copy in chunk_loads(step):
            copy.start()
    load(store_hbm, store, 2).start()

    barrier = pltpu.get_barrier_semaphore()
    partners = [{"tensor": lax.rem(z + step, depth)} for step in range(1, 4)]
    partners += [other_core, other_x, other_y]
    for partner in partners:
        pl.semaphore_signal(barrier, inc=1, device_id=partner, device_id_type=pl.DeviceIdType.MESH)

    def remote(source, target, send, recv, device):
        return pltpu.make_async_remote_copy(
            src_ref=source, dst_ref=target, send_sem=send, recv_sem=recv,
            device_id=device, device_id_type=pl.DeviceIdType.MESH,
        )

    def rs_copy(step):
        device = {"tensor": lax.rem(z + step, depth)}
        slot = step - 1
        return remote(part.at[slot], got.at[slot], rs_send.at[slot], rs_recv.at[slot], device)

    load(fi_hbm, fi, 0).wait()
    load(fo_hbm, fo, 1).wait()
    total = None
    for step in order:
        for copy in chunk_loads(step):
            copy.wait()
        summed = jnp.concatenate([dot_rows(qi[step], fi[...]), dot_rows(qg[step], fo[...])], axis=1)
        if step == 0:
            total = summed
            continue
        part[step - 1] = summed
        if step == order[0]:
            pl.semaphore_wait(barrier, len(partners))
        rs_copy(step).start()

    for step in (1, 2, 3):
        rs_copy(step).wait_recv()
        total = total + got[step - 1]

    turned[...] = total.T
    token = lax.broadcasted_iota(jnp.int32, (K // 2, rows), 1) // SEQ
    for half in range(2):
        picked = turned[pl.ds(K + half, K // 2, stride=2), :]
        for q in range(4):
            spread[half, pl.ds(q, K // 2, stride=4), :] = jnp.where(token == q, picked, 0.0)
    lane = lax.broadcasted_iota(jnp.int32, total.shape, 1)
    stacked = jnp.concatenate(
        [jnp.where(lane < K, total, 0.0), jnp.where(lane >= K, pltpu.roll(total, K, 1), 0.0)], axis=0
    )
    gradient = jnp.dot(jnp.concatenate([spread[0], spread[1]], axis=1), stacked, precision=HIGHEST, preferred_element_type=jnp.float32)

    def slot_of(yy, xx, zz, cc):
        return ((xx * 2 + cc) * 2 + yy) * depth + zz

    blocks[slot_of(y, x, z, core)] = gradient.astype(jnp.bfloat16)

    def move(slot, kind, zz, device):
        return remote(blocks.at[slot], blocks.at[slot], ag_send.at[kind, zz], ag_recv.at[slot], device)

    def arrived(slot):
        remote(blocks.at[slot], blocks.at[slot], ag_send.at[0, 0], ag_recv.at[slot], other_core).wait_recv()

    def column(zz, up, down):
        slot = slot_of(y, x, zz, core)

        @pl.when(jnp.logical_and(up, z < depth - 1))
        def _():
            move(slot, 0, zz, {"tensor": jnp.minimum(z + 1, depth - 1)}).start()

        @pl.when(jnp.logical_and(down, z > 0))
        def _():
            move(slot, 1, zz, {"tensor": jnp.maximum(z - 1, 0)}).start()

        move(slot, 2, zz, other_x).start()
        move(slot, 3, zz, other_y).start()
        move(slot, 4, zz, other_core).start()

    def neighbours(zz):
        along_x = slot_of(y, 1 - x, zz, core)
        along_y = slot_of(1 - y, x, zz, core)
        even = zz % 2 == 0
        arrived(along_x)

        @pl.when(even)
        def _():
            move(along_x, 8, zz, other_y).start()

        move(along_x, 5, zz, other_core).start()
        arrived(along_y)

        @pl.when(jnp.logical_not(even))
        def _():
            move(along_y, 8, zz, other_x).start()

        move(along_y, 6, zz, other_core).start()

    def at_distance(step, act):
        if step == 0:
            act(z, True, True)
            return

        @pl.when(z - step >= 0)
        def _():
            act(jnp.maximum(z - step, 0), True, False)

        @pl.when(z + step < depth)
        def _():
            act(jnp.minimum(z + step, depth - 1), False, True)

    def arrived_column(zz, up, down):
        arrived(slot_of(y, x, zz, core))
        column(zz, up, down)

    low = lax.broadcasted_iota(jnp.int32, (16, 8, 128), 1) < 4

    def regroup(yy, xx, cc):
        base = slot_of(yy, xx, 0, cc)
        evens, odds = [], []
        for pair in range(2):
            a = blocks[base + 2 * pair].astype(jnp.float32).reshape(16, 8, 128)
            b = blocks[base + 2 * pair + 1].astype(jnp.float32).reshape(16, 8, 128)
            evens.append(jnp.where(low, a, pltpu.roll(b, 4, 1)))
            odds.append(jnp.where(low, pltpu.roll(a, 4, 1), b))
        even = jnp.concatenate(evens, axis=1).astype(jnp.bfloat16)
        odd = jnp.concatenate(odds, axis=1).astype(jnp.bfloat16)
        start = pl.multiple_of(base * 4, 16)
        for m in range(16):
            wide[pl.ds(start, 16), m * 256 : m * 256 + 128] = even[m]
            wide[pl.ds(start, 16), m * 256 + 128 : (m + 1) * 256] = odd[m]

    column(z, True, True)
    for step in range(1, 4):
        at_distance(step, arrived_column)
        at_distance(step - 1, lambda zz, up, down: neighbours(zz))
    at_distance(3, lambda zz, up, down: neighbours(zz))
    regroup(y, x, core)
    regroup(y, 1 - x, core)
    regroup(1 - y, x, core)
    for zz in range(4):
        slot = slot_of(1 - y, 1 - x, zz, core)
        arrived(slot)
        move(slot, 7, zz, other_core).start()
    regroup(1 - y, 1 - x, core)
    for yy, xx in ((y, x), (y, 1 - x), (1 - y, x), (1 - y, 1 - x)):
        for zz in range(4):
            arrived(slot_of(yy, xx, zz, 1 - core))
        regroup(yy, xx, 1 - core)

    load(store_hbm, store, 2).wait()
    out_ref[...] = dot_rows(store[...], wide[...])

    for step in (1, 2, 3):
        rs_copy(step).wait_send()
    own = slot_of(y, x, z, core)

    def sent(kind, zz):
        move(own, kind, zz, other_core).wait_send()

    for zz in range(4):
        for kind in range(2, 9):
            sent(kind, zz)

        @pl.when(jnp.logical_and(zz <= z, z < depth - 1))
        def _():
            sent(0, zz)

        @pl.when(jnp.logical_and(zz >= z, z > 0))
        def _():
            sent(1, zz)


def fused(query_inputs, query_grads, input_factor, output_factor, train_store):
    tokens, width = query_inputs.shape
    hidden = query_grads.shape[1]
    rows = tokens // 8
    queries = 32 * 4
    any_spec = pl.BlockSpec(memory_space=pl.ANY)
    return pl.pallas_call(
        fused_kernel,
        out_shape=jax.ShapeDtypeStruct((train_store.shape[0], queries), jnp.float32),
        in_specs=[any_spec] * 5,
        out_specs=pl.BlockSpec(memory_space=pltpu.VMEM),
        scratch_shapes=[
            pltpu.VMEM((4, rows, width), jnp.bfloat16),
            pltpu.VMEM((4, rows, hidden), jnp.bfloat16),
            pltpu.VMEM(input_factor.shape, jnp.bfloat16),
            pltpu.VMEM(output_factor.shape, jnp.bfloat16),
            pltpu.VMEM(train_store.shape, jnp.bfloat16),
            pltpu.VMEM((3, rows, 2 * K), jnp.float32),
            pltpu.VMEM((3, rows, 2 * K), jnp.float32),
            pltpu.VMEM((2 * K, rows), jnp.float32),
            pltpu.VMEM((2, rows, rows), jnp.float32),
            pltpu.VMEM((32, rows, 2 * K), jnp.bfloat16),
            pltpu.VMEM((queries, K * K), jnp.bfloat16),
            pltpu.SemaphoreType.DMA((11,)),
            pltpu.SemaphoreType.DMA((3,)),
            pltpu.SemaphoreType.DMA((3,)),
            pltpu.SemaphoreType.DMA((9, 4)),
            pltpu.SemaphoreType.DMA((32,)),
        ],
        compiler_params=pltpu.CompilerParams(
            collective_id=0, has_side_effects=True, vmem_limit_bytes=40 * 1024 * 1024
        ),
        cost_estimate=pl.CostEstimate(flops=1_000_000_000, bytes_accessed=8_000_000, transcendentals=0),
    )(query_inputs, query_grads, input_factor, output_factor, train_store)


def from_behind(value, axis, steps):
    count = lax.axis_size(axis)
    pairs = [(source, (source + steps) % count) for source in range(count)]
    return lax.ppermute(value, axis, pairs)


def outer_blocks(inputs_rows, grads_rows):
    examples = inputs_rows.shape[0] // SEQ
    blocks = jnp.einsum(
        "eto,eti->eoi",
        grads_rows.reshape(examples, SEQ, K),
        inputs_rows.reshape(examples, SEQ, K),
        precision=HIGHEST,
    )
    return blocks.reshape(examples, K * K).astype(jnp.bfloat16)


def ring(query_inputs, query_grads, input_factor, output_factor, train_store):
    inputs_part = dot_rows(query_inputs, input_factor)
    grads_part = dot_rows(query_grads, output_factor)
    inputs_full, grads_full = lax.psum((inputs_part, grads_part), "tensor")
    block = outer_blocks(inputs_full, grads_full)

    def place_block(scores, piece, start):
        return lax.dynamic_update_slice_in_dim(scores, dot_rows(train_store, piece), start, 1)

    per_owner = block.shape[0]
    cycle_size = lax.axis_size("dp")
    own_index = lax.axis_index("dp")
    scores_empty = jnp.zeros((train_store.shape[0], per_owner * cycle_size), jnp.float32)
    scores = place_block(scores_empty, block, own_index * per_owner)

    def cycle_step(turn, carry):
        held, scores = carry
        held = from_behind(held, "dp", 1)
        owner = (own_index - turn) % cycle_size
        return (held, place_block(scores, held, owner * per_owner))

    held, scores = lax.fori_loop(1, cycle_size, cycle_step, (block, scores))
    return scores


def local(query_inputs, *rest):
    sizes = tuple(lax.axis_size(axis) for axis in ("groups", "dp", "tensor"))
    if sizes == (2, 4, 4) and query_inputs.shape[0] == 8 * 4 * SEQ:
        return fused(query_inputs, *rest)
    return ring(query_inputs, *rest)


def solution(mesh):
    return jax.shard_map(
        local,
        mesh=mesh,
        in_specs=(
            P("dp", "tensor"),
            P("dp", "tensor"),
            P(None, "tensor"),
            P(None, "tensor"),
            P(("groups", "dp", "tensor"), None),
        ),
        out_specs=P(("groups", "dp", "tensor"), None),
        check_vma=False,
    )
```

time: 108 us -> 41 us (0.38); the launches traced: 106 us -> 40.7 us
  waiting for transfers between devices: 64.6 us -> 0 us
  Pallas kernels: 0 us -> 31.8 us
  matrix products: 20 us -> 0 us
  between operations: 13.4 us -> 0.01 us
  local copies, waits for them, and re-layouts: 1.29 us -> 8.92 us
  starting transfers between devices: 6.66 us -> 0 us
    psum x1 -> x0, waiting for transfers between devices: 54.6 us -> none  [local(): inputs_full, grads_full = lax.psum((inputs_part, grads_part), 'tensor')]
    pallas_call x0 -> x1, Pallas kernels: none -> 31.8 us  [fused(): pl.pallas_call(fused_kernel, out_shape=jax.ShapeDtypeStruct((train_store....]
    dot_general x7 -> x0, matrix products: 20 us -> none  [the longest x4 9.27 us: score_piece(): lax.dot_general(train_store, piece, (((1,), (1,)), ((), ())), preferred_e...]
    ppermute x3 -> x0, waiting for transfers between devices: 9.95 us -> none  [from_behind(): return lax.ppermute(value, axis, pairs)]
    unnamed x4 -> x11, local copies, waits for them, and re-layouts: 0.01 us -> 8.92 us
    ppermute x3 -> x0, starting transfers between devices: 6.66 us -> none  [from_behind(): return lax.ppermute(value, axis, pairs)]
  transfers between devices with their start and end apart: 4 -> 0, of which waited for: 4 -> 0; matrix products, arithmetic and copies ran while one was open for 0% -> 0% of each run, Pallas kernels for 0% -> 0%
where the time goes in v1:
time: 41 us; the launch traced here: 40.7 us
  Pallas kernels  31.8 us (78%)
  local copies, waits for them, and re-layouts  8.92 us (22%)
    pallas_call x1, Pallas kernels, fused(): pl.pallas_call(fused_kernel, out_shape=jax.ShapeDtypeStruct((train_store....  31.8 us
    unnamed x11, local copies, waits for them, and re-layouts  8.92 us

profile of v1, /device:TPU:1, one launch (start us, length us, event | category | flops | bytes accessed | tf_op | source)
XLA Modules:
  0.0 40.7 jit_solution(14291411518377002025)
XLA Ops:
  0.0 0.0 copy-start
  0.0 3.0 %copy-done = bf16[1024,3456]{1,0:T(8,128)(2,1)S(1)} copy-done((bf16[1024,3456]{1,0:T(8,128)(2,1)S(1)}, bf16[1024,3456]{1,0:T(8,128)(2,1)}, u32[]{:S(2)}) %copy-start) | copy-done | bytes 7077912
  3.0 0.0 copy-start.1
  3.0 1.7 %copy-done.1 = bf16[1024,1280]{1,0:T(8,128)(2,1)S(1)} copy-done((bf16[1024,1280]{1,0:T(8,128)(2,1)S(1)}, bf16[1024,1280]{1,0:T(8,128)(2,1)}, u32[]{:S(2)}) %copy-start.1) | copy-done | bytes 2621464
  4.8 0.0 copy-start.2
  4.8 1.6 %copy-done.2 = bf16[256,4096]{1,0:T(8,128)(2,1)S(1)} copy-done((bf16[256,4096]{1,0:T(8,128)(2,1)S(1)}, bf16[256,4096]{1,0:T(8,128)(2,1)}, u32[]{:S(2)}) %copy-start.2) | copy-done | bytes 2097176
  6.3 0.0 copy-start.3
  6.3 1.0 %copy-done.3 = bf16[64,3456]{1,0:T(8,128)(2,1)S(1)} copy-done((bf16[64,3456]{1,0:T(8,128)(2,1)S(1)}, bf16[64,3456]{1,0:T(8,128)(2,1)}, u32[]{:S(2)}) %copy-start.3) | copy-done | bytes 442392
  7.4 0.0 copy-start.4
  7.4 0.9 %copy-done.4 = bf16[64,1280]{1,0:T(8,128)(2,1)S(1)} copy-done((bf16[64,1280]{1,0:T(8,128)(2,1)S(1)}, bf16[64,1280]{1,0:T(8,128)(2,1)}, u32[]{:S(2)}) %copy-start.4) | copy-done | bytes 163864
  8.3 31.8 %shard_map.55 = f32[256,128]{1,0:T(8,128)S(1)} custom-call(bf16[1024,1280]{1,0:T(8,128)(2,1)S(1)} %copy-done.1, bf16[1024,3456]{1,0:T(8,128)(2,1)S(1)} %copy-done, bf16[64,1280]{1,0:T(8,128)(2,1)S(1)} %copy-done.4, bf16[64,3456]{1,0:T(8,128)(2,1)S(1)} %copy-done.3, bf16[256,4096]{1,0:T(8,128)(2,1)S(1)} %copy-done.2), custom_call_target="tpu_custom_call" | custom-call | flops 1000000000 | bytes 8000000 | tf_op jit(solution)/shard_map/pallas_call | solution.py:226
  40.1 0.7 %copy.7 = f32[256,128]{1,0:T(8,128)} copy(f32[256,128]{1,0:T(8,128)S(1)} %shard_map.55) | data formatting | bytes 262144
Async XLA Ops:
  0.0 3.0 %copy-start = (bf16[1024,3456]{1,0:T(8,128)(2,1)S(1)}, bf16[1024,3456]{1,0:T(8,128)(2,1)}, u32[]{:S(2)}) copy-start(bf16[1024,3456]{1,0:T(8,128)(2,1)} %qg_hbm.1) | copy-start | bytes 21233668
  3.0 1.7 %copy-start.1 = (bf16[1024,1280]{1,0:T(8,128)(2,1)S(1)}, bf16[1024,1280]{1,0:T(8,128)(2,1)}, u32[]{:S(2)}) copy-start(bf16[1024,1280]{1,0:T(8,128)(2,1)} %qi_hbm.1) | copy-start | bytes 7864324
  4.8 1.6 %copy-start.2 = (bf16[256,4096]{1,0:T(8,128)(2,1)S(1)}, bf16[256,4096]{1,0:T(8,128)(2,1)}, u32[]{:S(2)}) copy-start(bf16[256,4096]{1,0:T(8,128)(2,1)} %store_hbm.1) | copy-start | bytes 6291460
  6.3 1.0 %copy-start.3 = (bf16[64,3456]{1,0:T(8,128)(2,1)S(1)}, bf16[64,3456]{1,0:T(8,128)(2,1)}, u32[]{:S(2)}) copy-start(bf16[64,3456]{1,0:T(8,128)(2,1)} %fo_hbm.1) | copy-start | bytes 1327108
  7.4 0.9 %copy-start.4 = (bf16[64,1280]{1,0:T(8,128)(2,1)S(1)}, bf16[64,1280]{1,0:T(8,128)(2,1)}, u32[]{:S(2)}) copy-start(bf16[64,1280]{1,0:T(8,128)(2,1)} %fi_hbm.1) | copy-start | bytes 491524

commit v2 on v1

--- a/solution.py
+++ b/solution.py
@@ -29,14 +29,17 @@
     other_core = {"dp": x * 2 + (1 - core)}
     other_x = {"dp": (1 - x) * 2 + core}
     other_y = {"groups": 1 - y}
-    order = (2, 1, 3, 0)
+    other_xy = {"groups": 1 - y, "dp": (1 - x) * 2 + core}
+    order = (2, 3, 1, 0)
+
+    def peer(step):
+        return (z, z + 1 - 2 * (z % 2), lax.rem(z + 2, depth), depth - 1 - z)[step]
 
     def load(source, target, index):
         return pltpu.make_async_copy(source, target, load_sem.at[index])
 
     def chunk_loads(step):
-        target = lax.rem(z + step, depth)
-        start = pl.multiple_of((y * depth + target) * rows, rows)
+        start = pl.multiple_of((y * depth + peer(step)) * rows, rows)
         return (
             load(qi_hbm.at[pl.ds(start, rows), :], qi.at[step], 3 + 2 * step),
             load(qg_hbm.at[pl.ds(start, rows), :], qg.at[step], 4 + 2 * step),
@@ -50,8 +53,8 @@
     load(store_hbm, store, 2).start()
 
     barrier = pltpu.get_barrier_semaphore()
-    partners = [{"tensor": lax.rem(z + step, depth)} for step in range(1, 4)]
-    partners += [other_core, other_x, other_y]
+    partners = [{"tensor": peer(step)} for step in range(1, 4)]
+    partners += [other_core, other_x, other_y, other_xy]
     for partner in partners:
         pl.semaphore_signal(barrier, inc=1, device_id=partner, device_id_type=pl.DeviceIdType.MESH)
 
@@ -62,7 +65,7 @@
         )
 
     def rs_copy(step):
-        device = {"tensor": lax.rem(z + step, depth)}
+        device = {"tensor": peer(step)}
         slot = step - 1
         return remote(part.at[slot], got.at[slot], rs_send.at[slot], rs_recv.at[slot], device)
 
@@ -108,56 +111,20 @@
     def arrived(slot):
         remote(blocks.at[slot], blocks.at[slot], ag_send.at[0, 0], ag_recv.at[slot], other_core).wait_recv()
 
-    def column(zz, up, down):
+    def column(step):
+        zz = peer(step)
         slot = slot_of(y, x, zz, core)
-
-        @pl.when(jnp.logical_and(up, z < depth - 1))
-        def _():
-            move(slot, 0, zz, {"tensor": jnp.minimum(z + 1, depth - 1)}).start()
-
-        @pl.when(jnp.logical_and(down, z > 0))
-        def _():
-            move(slot, 1, zz, {"tensor": jnp.maximum(z - 1, 0)}).start()
-
-        move(slot, 2, zz, other_x).start()
-        move(slot, 3, zz, other_y).start()
-        move(slot, 4, zz, other_core).start()
-
-    def neighbours(zz):
-        along_x = slot_of(y, 1 - x, zz, core)
-        along_y = slot_of(1 - y, x, zz, core)
-        even = zz % 2 == 0
-        arrived(along_x)
-
-        @pl.when(even)
-        def _():
-            move(along_x, 8, zz, other_y).start()
-
-        move(along_x, 5, zz, other_core).start()
-        arrived(along_y)
-
-        @pl.when(jnp.logical_not(even))
-        def _():
-            move(along_y, 8, zz, other_x).start()
-
-        move(along_y, 6, zz, other_core).start()
-
-    def at_distance(step, act):
-        if step == 0:
-            act(z, True, True)
-            return
-
-        @pl.when(z - step >= 0)
-        def _():
-            act(jnp.maximum(z - step, 0), True, False)
-
-        @pl.when(z + step < depth)
-        def _():
-            act(jnp.minimum(z + step, depth - 1), False, True)
-
-    def arrived_column(zz, up, down):
-        arrived(slot_of(y, x, zz, core))
-        column(zz, up, down)
+        if step:
+            arrived(slot)
+        for kind, device in enumerate((other_xy, other_x, other_y, other_core)):
+            move(slot, kind, zz, device).start()
+
+    def plane(step):
+        zz = peer(step)
+        for kind, (yy, xx) in enumerate(((y, 1 - x), (1 - y, x), (1 - y, 1 - x))):
+            slot = slot_of(yy, xx, zz, core)
+            arrived(slot)
+            move(slot, 4 + kind, zz, other_core).start()
 
     low = lax.broadcasted_iota(jnp.int32, (16, 8, 128), 1) < 4
 
@@ -176,18 +143,15 @@
             wide[pl.ds(start, 16), m * 256 : m * 256 + 128] = even[m]
             wide[pl.ds(start, 16), m * 256 + 128 : (m + 1) * 256] = odd[m]
 
-    column(z, True, True)
-    for step in range(1, 4):
-        at_distance(step, arrived_column)
-        at_distance(step - 1, lambda zz, up, down: neighbours(zz))
-    at_distance(3, lambda zz, up, down: neighbours(zz))
+    for step in (2, 3, 1):
+        move(slot_of(y, x, z, core), 6 + step, z, {"tensor": peer(step)}).start()
+    for step in (0, 1, 3, 2):
+        column(step)
     regroup(y, x, core)
+    for step in (0, 1, 3, 2):
+        plane(step)
     regroup(y, 1 - x, core)
     regroup(1 - y, x, core)
-    for zz in range(4):
-        slot = slot_of(1 - y, 1 - x, zz, core)
-        arrived(slot)
-        move(slot, 7, zz, other_core).start()
     regroup(1 - y, 1 - x, core)
     for yy, xx in ((y, x), (y, 1 - x), (1 - y, x), (1 - y, 1 - x)):
         for zz in range(4):
@@ -201,20 +165,11 @@
         rs_copy(step).wait_send()
     own = slot_of(y, x, z, core)
 
-    def sent(kind, zz):
-        move(own, kind, zz, other_core).wait_send()
-
     for zz in range(4):
-        for kind in range(2, 9):
-            sent(kind, zz)
-
-        @pl.when(jnp.logical_and(zz <= z, z < depth - 1))
-        def _():
-            sent(0, zz)
-
-        @pl.when(jnp.logical_and(zz >= z, z > 0))
-        def _():
-            sent(1, zz)
+        for kind in range(7):
+            move(own, kind, zz, other_core).wait_send()
+    for step in (1, 2, 3):
+        move(own, 6 + step, z, other_core).wait_send()
 
 
 def fused(query_inputs, query_grads, input_factor, output_factor, train_store):
@@ -243,11 +198,11 @@
             pltpu.SemaphoreType.DMA((11,)),
             pltpu.SemaphoreType.DMA((3,)),
             pltpu.SemaphoreType.DMA((3,)),
-            pltpu.SemaphoreType.DMA((9, 4)),
+            pltpu.SemaphoreType.DMA((10, 4)),
             pltpu.SemaphoreType.DMA((32,)),
         ],
         compiler_params=pltpu.CompilerParams(
-            collective_id=0, has_side_effects=True, vmem_limit_bytes=40 * 1024 * 1024
+            collective_id=0, has_side_effects=True, vmem_limit_bytes=60 * 1024 * 1024
         ),
         cost_estimate=pl.CostEstimate(flops=1_000_000_000, bytes_accessed=8_000_000, transcendentals=0),
     )(query_inputs, query_grads, input_factor, output_factor, train_store)

time: 41 us -> 26.6 us (0.65)
  local copies, waits for them, and re-layouts: 8.92 us -> 1.57 us
  Pallas kernels: 31.8 us -> 24.9 us
    unnamed x11 -> x1, local copies, waits for them, and re-layouts: 8.92 us -> 1.57 us
    pallas_call x1, Pallas kernels: 31.8 us -> 24.9 us  [fused(): pl.pallas_call(fused_kernel, out_shape=jax.ShapeDtypeStruct((train_store....]
where the time goes in v2:
time: 26.6 us; the launch traced here: 26.5 us
  Pallas kernels  24.9 us (94%)
  local copies, waits for them, and re-layouts  1.57 us (6%)
    pallas_call x1, Pallas kernels, fused(): pl.pallas_call(fused_kernel, out_shape=jax.ShapeDtypeStruct((train_store....  24.9 us
    unnamed x1, local copies, waits for them, and re-layouts  1.57 us

profile of v2, /device:TPU:1, one launch (start us, length us, event | category | flops | bytes accessed | tf_op | source)
XLA Modules:
  0.0 26.5 jit_solution(250071520521798328)
XLA Ops:
  0.0 24.9 %shard_map.55 = f32[256,128]{1,0:T(8,128)} custom-call(bf16[1024,1280]{1,0:T(8,128)(2,1)} %qi_hbm.1, bf16[1024,3456]{1,0:T(8,128)(2,1)} %qg_hbm.1, bf16[64,1280]{1,0:T(8,128)(2,1)} %fi_hbm.1, bf16[64,3456]{1,0:T(8,128)(2,1)} %fo_hbm.1, bf16[256,4096]{1,0:T(8,128)(2,1)} %store_hbm.1), custom_call_target="tpu_custom_call" | custom-call | flops 1000000000 | bytes 8000000 | tf_op jit(solution)/shard_map/pallas_call | solution.py:181
  24.9 1.6 %copy.7 = f32[256,128]{1,0:T(8,128)} copy(f32[256,128]{1,0:T(8,128)} %shard_map.55) | data formatting | bytes 262144

commit v3 on v2

--- a/solution.py
+++ b/solution.py
@@ -17,7 +17,7 @@
 def fused_kernel(
     qi_hbm, qg_hbm, fi_hbm, fo_hbm, store_hbm, out_ref,
     qi, qg, fi, fo, store, part, got, turned, spread, blocks, wide,
-    load_sem, rs_send, rs_recv, ag_send, ag_recv,
+    load_sem, rs_send, rs_recv, ag_send, ag_recv, group_recv,
 ):
     depth = lax.axis_size("tensor")
     rows = qi.shape[1]
@@ -30,7 +30,8 @@
     other_x = {"dp": (1 - x) * 2 + core}
     other_y = {"groups": 1 - y}
     other_xy = {"groups": 1 - y, "dp": (1 - x) * 2 + core}
-    order = (2, 3, 1, 0)
+    order = (3, 2, 1, 0)
+    half = rows // 2
 
     def peer(step):
         return (z, z + 1 - 2 * (z % 2), lax.rem(z + 2, depth), depth - 1 - z)[step]
@@ -64,112 +65,130 @@
             device_id=device, device_id_type=pl.DeviceIdType.MESH,
         )
 
-    def rs_copy(step):
-        device = {"tensor": peer(step)}
-        slot = step - 1
-        return remote(part.at[slot], got.at[slot], rs_send.at[slot], rs_recv.at[slot], device)
+    def sums(kind):
+        source, step = (
+            (part.at[3, pl.ds(half, half)], 1),
+            (part.at[3, pl.ds(0, half)], 3),
+            (part.at[2, pl.ds(0, half)], 2),
+            (part.at[1, pl.ds(0, half)], 1),
+            (part.at[1, pl.ds(half, half)], 1),
+            (part.at[2, pl.ds(half, half)], 2),
+        )[kind]
+        return remote(source, got.at[kind], rs_send.at[kind], rs_recv.at[kind], {"tensor": peer(step)})
 
     load(fi_hbm, fi, 0).wait()
     load(fo_hbm, fo, 1).wait()
-    total = None
     for step in order:
         for copy in chunk_loads(step):
             copy.wait()
-        summed = jnp.concatenate([dot_rows(qi[step], fi[...]), dot_rows(qg[step], fo[...])], axis=1)
-        if step == 0:
-            total = summed
-            continue
-        part[step - 1] = summed
+        part[step] = jnp.concatenate([dot_rows(qi[step], fi[...]), dot_rows(qg[step], fo[...])], axis=1)
         if step == order[0]:
             pl.semaphore_wait(barrier, len(partners))
-        rs_copy(step).start()
-
-    for step in (1, 2, 3):
-        rs_copy(step).wait_recv()
-        total = total + got[step - 1]
-
-    turned[...] = total.T
-    token = lax.broadcasted_iota(jnp.int32, (K // 2, rows), 1) // SEQ
-    for half in range(2):
-        picked = turned[pl.ds(K + half, K // 2, stride=2), :]
-        for q in range(4):
-            spread[half, pl.ds(q, K // 2, stride=4), :] = jnp.where(token == q, picked, 0.0)
-    lane = lax.broadcasted_iota(jnp.int32, total.shape, 1)
-    stacked = jnp.concatenate(
-        [jnp.where(lane < K, total, 0.0), jnp.where(lane >= K, pltpu.roll(total, K, 1), 0.0)], axis=0
-    )
-    gradient = jnp.dot(jnp.concatenate([spread[0], spread[1]], axis=1), stacked, precision=HIGHEST, preferred_element_type=jnp.float32)
+        for kind in ((), (3, 4), (2,), (0, 1))[step]:
+            sums(kind).start()
+
+    sums(0).wait_recv()
+    part[2, half:] = part[2, half:] + got[0]
+    sums(5).start()
+
+    lane = lax.broadcasted_iota(jnp.int32, (half, 2 * K), 1)
+    lane8 = lax.broadcasted_iota(jnp.int32, (8, 2 * half), 1)
+
+    def query_gradients(total):
+        turned[...] = jnp.concatenate([total, total], axis=0).T
+        for place, pair in enumerate((0, 2, 1, 3)):
+            first = turned[pl.ds(K + 2 * pair, 8, stride=8), :]
+            second = turned[pl.ds(K + 2 * pair + 1, 8, stride=8), :]
+            both = jnp.where(lane8 < half, first, second)
+            for q in range(2):
+                spread[pl.ds(place * 2 + q, 8, stride=8), :] = jnp.where((lane8 % half) // SEQ == q, both, 0.0)
+        stacked = jnp.concatenate(
+            [jnp.where(lane < K, total, 0.0), jnp.where(lane >= K, pltpu.roll(total, K, 1), 0.0)], axis=0
+        )
+        product = jnp.dot(spread[...], stacked, precision=HIGHEST, preferred_element_type=jnp.float32)
+        return product.astype(jnp.bfloat16)
 
     def slot_of(yy, xx, zz, cc):
         return ((xx * 2 + cc) * 2 + yy) * depth + zz
 
-    blocks[slot_of(y, x, z, core)] = gradient.astype(jnp.bfloat16)
-
-    def move(slot, kind, zz, device):
-        return remote(blocks.at[slot], blocks.at[slot], ag_send.at[kind, zz], ag_recv.at[slot], device)
-
-    def arrived(slot):
-        remote(blocks.at[slot], blocks.at[slot], ag_send.at[0, 0], ag_recv.at[slot], other_core).wait_recv()
-
-    def column(step):
+    def move(part_of, slot, kind, zz, device):
+        block = blocks.at[part_of * 32 + slot]
+        recv = group_recv.at[part_of, slot // depth] if kind < 3 else ag_recv.at[part_of, zz]
+        return remote(block, block, ag_send, recv, device)
+
+    def four(part_of, yy, xx, cc):
+        base = slot_of(yy, xx, 0, cc)
+        blocks_of = blocks.at[pl.ds(part_of * 32 + base, 4)]
+        return remote(blocks_of, blocks_of, ag_send, group_recv.at[part_of, base // depth], other_core)
+
+    def column(part_of, step):
         zz = peer(step)
         slot = slot_of(y, x, zz, core)
         if step:
-            arrived(slot)
-        for kind, device in enumerate((other_xy, other_x, other_y, other_core)):
-            move(slot, kind, zz, device).start()
-
-    def plane(step):
-        zz = peer(step)
-        for kind, (yy, xx) in enumerate(((y, 1 - x), (1 - y, x), (1 - y, 1 - x))):
-            slot = slot_of(yy, xx, zz, core)
-            arrived(slot)
-            move(slot, 4 + kind, zz, other_core).start()
-
-    low = lax.broadcasted_iota(jnp.int32, (16, 8, 128), 1) < 4
+            move(part_of, slot, 3, zz, other_core).wait_recv()
+        for kind, device in enumerate((other_xy, other_x, other_y)):
+            move(part_of, slot, kind, zz, device).start()
+
+    row8 = lax.broadcasted_iota(jnp.int32, (8, 8, 2 * K), 1)
+    low = row8 < 4
+    first_of_two = (row8 // 2) % 2 == 0
+
+    def pairs(slot):
+        a = blocks[slot].astype(jnp.float32).reshape(8, 8, 2 * K)
+        b = blocks[32 + slot].astype(jnp.float32).reshape(8, 8, 2 * K)
+        return jnp.where(first_of_two, a, pltpu.roll(b, 2, 1)), jnp.where(first_of_two, pltpu.roll(a, 6, 1), b)
 
     def regroup(yy, xx, cc):
         base = slot_of(yy, xx, 0, cc)
-        evens, odds = [], []
-        for pair in range(2):
-            a = blocks[base + 2 * pair].astype(jnp.float32).reshape(16, 8, 128)
-            b = blocks[base + 2 * pair + 1].astype(jnp.float32).reshape(16, 8, 128)
-            evens.append(jnp.where(low, a, pltpu.roll(b, 4, 1)))
-            odds.append(jnp.where(low, pltpu.roll(a, 4, 1), b))
-        even = jnp.concatenate(evens, axis=1).astype(jnp.bfloat16)
-        odd = jnp.concatenate(odds, axis=1).astype(jnp.bfloat16)
         start = pl.multiple_of(base * 4, 16)
-        for m in range(16):
-            wide[pl.ds(start, 16), m * 256 : m * 256 + 128] = even[m]
-            wide[pl.ds(start, 16), m * 256 + 128 : (m + 1) * 256] = odd[m]
-
-    for step in (2, 3, 1):
-        move(slot_of(y, x, z, core), 6 + step, z, {"tensor": peer(step)}).start()
-    for step in (0, 1, 3, 2):
-        column(step)
-    regroup(y, x, core)
-    for step in (0, 1, 3, 2):
-        plane(step)
-    regroup(y, 1 - x, core)
-    regroup(1 - y, x, core)
-    regroup(1 - y, 1 - x, core)
-    for yy, xx in ((y, x), (y, 1 - x), (1 - y, x), (1 - y, 1 - x)):
-        for zz in range(4):
-            arrived(slot_of(yy, xx, zz, 1 - core))
-        regroup(yy, xx, 1 - core)
+        held = [pairs(base + zz) for zz in range(4)]
+        for e in range(2):
+            evens, odds = [], []
+            for zz in (0, 2):
+                a, b = held[zz][e], held[zz + 1][e]
+                evens.append(jnp.where(low, a, pltpu.roll(b, 4, 1)))
+                odds.append(jnp.where(low, pltpu.roll(a, 4, 1), b))
+            even = jnp.concatenate(evens, axis=1).astype(jnp.bfloat16)
+            odd = jnp.concatenate(odds, axis=1).astype(jnp.bfloat16)
+            for g in range(8):
+                at = (2 * g + e) * 256
+                wide[pl.ds(start, 16), at : at + 128] = even[g]
+                wide[pl.ds(start, 16), at + 128 : at + 256] = odd[g]
+
+    own = slot_of(y, x, z, core)
+    for part_of, kinds in ((0, (3, 1, 2)), (1, (4, 5))):
+        total = part[0, part_of * half : (part_of + 1) * half]
+        for kind in kinds:
+            sums(kind).wait_recv()
+            total = total + got[kind]
+        blocks[part_of * 32 + own] = query_gradients(total)
+        for step in (2, 3, 1):
+            move(part_of, own, 3, z, {"tensor": peer(step)}).start()
+        column(part_of, 0)
+
+    for part_of in range(2):
+        for step in (1, 3, 2):
+            column(part_of, step)
+        four(part_of, y, x, core).start()
+    chips = ((y, x), (y, 1 - x), (1 - y, x), (1 - y, 1 - x))
+    for part_of in range(2):
+        for yy, xx in chips[1:]:
+            four(part_of, yy, xx, core).wait_recv()
+            four(part_of, yy, xx, core).start()
+    for cc in (core, 1 - core):
+        for yy, xx in chips:
+            if cc is not core:
+                for part_of in range(2):
+                    four(part_of, yy, xx, cc).wait_recv()
+            regroup(yy, xx, cc)
 
     load(store_hbm, store, 2).wait()
     out_ref[...] = dot_rows(store[...], wide[...])
 
-    for step in (1, 2, 3):
-        rs_copy(step).wait_send()
-    own = slot_of(y, x, z, core)
-
-    for zz in range(4):
-        for kind in range(7):
-            move(own, kind, zz, other_core).wait_send()
-    for step in (1, 2, 3):
-        move(own, 6 + step, z, other_core).wait_send()
+    for kind in range(6):
+        sums(kind).wait_send()
+    every = blocks.at[pl.ds(0, 62)]
+    remote(every, every, ag_send, ag_recv.at[0, z], other_core).wait_send()
 
 
 def fused(query_inputs, query_grads, input_factor, output_factor, train_store):
@@ -189,17 +208,18 @@
             pltpu.VMEM(input_factor.shape, jnp.bfloat16),
             pltpu.VMEM(output_factor.shape, jnp.bfloat16),
             pltpu.VMEM(train_store.shape, jnp.bfloat16),
-            pltpu.VMEM((3, rows, 2 * K), jnp.float32),
-            pltpu.VMEM((3, rows, 2 * K), jnp.float32),
+            pltpu.VMEM((4, rows, 2 * K), jnp.float32),
+            pltpu.VMEM((6, rows // 2, 2 * K), jnp.float32),
             pltpu.VMEM((2 * K, rows), jnp.float32),
-            pltpu.VMEM((2, rows, rows), jnp.float32),
-            pltpu.VMEM((32, rows, 2 * K), jnp.bfloat16),
+            pltpu.VMEM((rows // 2, rows), jnp.float32),
+            pltpu.VMEM((64, rows // 2, 2 * K), jnp.bfloat16),
             pltpu.VMEM((queries, K * K), jnp.bfloat16),
             pltpu.SemaphoreType.DMA((11,)),
-            pltpu.SemaphoreType.DMA((3,)),
-            pltpu.SemaphoreType.DMA((3,)),
-            pltpu.SemaphoreType.DMA((10, 4)),
-            pltpu.SemaphoreType.DMA((32,)),
+            pltpu.SemaphoreType.DMA((6,)),
+            pltpu.SemaphoreType.DMA((6,)),
+            pltpu.SemaphoreType.DMA,
+            pltpu.SemaphoreType.DMA((2, 4)),
+            pltpu.SemaphoreType.DMA((2, 8)),
         ],
         compiler_params=pltpu.CompilerParams(
             collective_id=0, has_side_effects=True, vmem_limit_bytes=60 * 1024 * 1024

time: 26.6 us -> 25.1 us (0.944)
  Pallas kernels: 24.9 us -> 23.4 us
    pallas_call x1, Pallas kernels: 24.9 us -> 23.4 us  [fused(): pl.pallas_call(fused_kernel, out_shape=jax.ShapeDtypeStruct((train_store....]
where the time goes in v3:
time: 25.1 us; the launch traced here: 25 us
  Pallas kernels  23.4 us (93%)
  local copies, waits for them, and re-layouts  1.57 us (6%)
    pallas_call x1, Pallas kernels, fused(): pl.pallas_call(fused_kernel, out_shape=jax.ShapeDtypeStruct((train_store....  23.4 us
    unnamed x1, local copies, waits for them, and re-layouts  1.57 us

profile of v3, /device:TPU:1, one launch (start us, length us, event | category | flops | bytes accessed | tf_op | source)
XLA Modules:
  0.0 25.0 jit_solution(1279146108868722871)
XLA Ops:
  0.0 23.4 %shard_map.55 = f32[256,128]{1,0:T(8,128)} custom-call(bf16[1024,1280]{1,0:T(8,128)(2,1)} %qi_hbm.1, bf16[1024,3456]{1,0:T(8,128)(2,1)} %qg_hbm.1, bf16[64,1280]{1,0:T(8,128)(2,1)} %fi_hbm.1, bf16[64,3456]{1,0:T(8,128)(2,1)} %fo_hbm.1, bf16[256,4096]{1,0:T(8,128)(2,1)} %store_hbm.1), custom_call_target="tpu_custom_call" | custom-call | flops 1000000000 | bytes 8000000 | tf_op jit(solution)/shard_map/pallas_call | solution.py:200
  23.4 1.6 %copy.7 = f32[256,128]{1,0:T(8,128)} copy(f32[256,128]{1,0:T(8,128)} %shard_map.55) | data formatting | bytes 262144

commit v4 on v3

--- a/solution.py
+++ b/solution.py
@@ -222,7 +222,7 @@
             pltpu.SemaphoreType.DMA((2, 8)),
         ],
         compiler_params=pltpu.CompilerParams(
-            collective_id=0, has_side_effects=True, vmem_limit_bytes=60 * 1024 * 1024
+            collective_id=0, has_side_effects=True, vmem_limit_bytes=55000 * 1024
         ),
         cost_estimate=pl.CostEstimate(flops=1_000_000_000, bytes_accessed=8_000_000, transcendentals=0),
     )(query_inputs, query_grads, input_factor, output_factor, train_store)

time: 25.1 us -> 23.6 us (0.940)
  local copies, waits for them, and re-layouts: 1.57 us -> 0.66 us
  Pallas kernels: 23.4 us -> 22.8 us
    unnamed x1, local copies, waits for them, and re-layouts: 1.57 us -> 0.66 us
    pallas_call x1, Pallas kernels: 23.4 us -> 22.8 us  [fused(): pl.pallas_call(fused_kernel, out_shape=jax.ShapeDtypeStruct((train_store....]
where the time goes in v4:
time: 23.6 us; the launch traced here: 23.4 us
  Pallas kernels  22.8 us (97%)
  local copies, waits for them, and re-layouts  0.66 us (3%)
    pallas_call x1, Pallas kernels, fused(): pl.pallas_call(fused_kernel, out_shape=jax.ShapeDtypeStruct((train_store....  22.8 us
    unnamed x1, local copies, waits for them, and re-layouts  0.66 us

profile of v4, /device:TPU:1, one launch (start us, length us, event | category | flops | bytes accessed | tf_op | source)
XLA Modules:
  0.0 23.4 jit_solution(13148729075531316531)
XLA Ops:
  0.0 22.8 %shard_map.55 = f32[256,128]{1,0:T(8,128)S(1)} custom-call(bf16[1024,1280]{1,0:T(8,128)(2,1)} %qi_hbm.1, bf16[1024,3456]{1,0:T(8,128)(2,1)} %qg_hbm.1, bf16[64,1280]{1,0:T(8,128)(2,1)} %fi_hbm.1, bf16[64,3456]{1,0:T(8,128)(2,1)} %fo_hbm.1, bf16[256,4096]{1,0:T(8,128)(2,1)} %store_hbm.1), custom_call_target="tpu_custom_call" | custom-call | flops 1000000000 | bytes 8000000 | tf_op jit(solution)/shard_map/pallas_call | solution.py:200
  22.8 0.7 %copy.7 = f32[256,128]{1,0:T(8,128)} copy(f32[256,128]{1,0:T(8,128)S(1)} %shard_map.55) | data formatting | bytes 262144

commit v5 on v4

--- a/solution.py
+++ b/solution.py
@@ -46,9 +46,12 @@
             load(qg_hbm.at[pl.ds(start, rows), :], qg.at[step], 4 + 2 * step),
         )
 
+    first_inputs, first_grads = chunk_loads(order[0])
     load(fi_hbm, fi, 0).start()
+    first_inputs.start()
     load(fo_hbm, fo, 1).start()
-    for step in order:
+    first_grads.start()
+    for step in order[1:]:
         for copy in chunk_loads(step):
             copy.start()
     load(store_hbm, store, 2).start()
@@ -77,11 +80,14 @@
         return remote(source, got.at[kind], rs_send.at[kind], rs_recv.at[kind], {"tensor": peer(step)})
 
     load(fi_hbm, fi, 0).wait()
-    load(fo_hbm, fo, 1).wait()
     for step in order:
-        for copy in chunk_loads(step):
-            copy.wait()
-        part[step] = jnp.concatenate([dot_rows(qi[step], fi[...]), dot_rows(qg[step], fo[...])], axis=1)
+        inputs_loaded, grads_loaded = chunk_loads(step)
+        inputs_loaded.wait()
+        projected_inputs = dot_rows(qi[step], fi[...])
+        if step == order[0]:
+            load(fo_hbm, fo, 1).wait()
+        grads_loaded.wait()
+        part[step] = jnp.concatenate([projected_inputs, dot_rows(qg[step], fo[...])], axis=1)
         if step == order[0]:
             pl.semaphore_wait(barrier, len(partners))
         for kind in ((), (3, 4), (2,), (0, 1))[step]:
@@ -162,12 +168,12 @@
             sums(kind).wait_recv()
             total = total + got[kind]
         blocks[part_of * 32 + own] = query_gradients(total)
-        for step in (2, 3, 1):
+        for step in (3, 2, 1):
             move(part_of, own, 3, z, {"tensor": peer(step)}).start()
         column(part_of, 0)
 
     for part_of in range(2):
-        for step in (1, 3, 2):
+        for step in (1, 2, 3):
             column(part_of, step)
         four(part_of, y, x, core).start()
     chips = ((y, x), (y, 1 - x), (1 - y, x), (1 - y, 1 - x))

time: 23.6 us -> 23.1 us (0.979)
  Pallas kernels: 22.8 us -> 22.3 us
    pallas_call x1, Pallas kernels: 22.8 us -> 22.3 us  [fused(): pl.pallas_call(fused_kernel, out_shape=jax.ShapeDtypeStruct((train_store....]
where the time goes in v5:
time: 23.1 us; the launch traced here: 22.9 us
  Pallas kernels  22.3 us (97%)
  local copies, waits for them, and re-layouts  0.66 us (3%)
    pallas_call x1, Pallas kernels, fused(): pl.pallas_call(fused_kernel, out_shape=jax.ShapeDtypeStruct((train_store....  22.3 us
    unnamed x1, local copies, waits for them, and re-layouts  0.66 us

profile of v5, /device:TPU:1, one launch (start us, length us, event | category | flops | bytes accessed | tf_op | source)
XLA Modules:
  0.0 22.9 jit_solution(18015292145418463780)
XLA Ops:
  0.0 22.3 %shard_map.55 = f32[256,128]{1,0:T(8,128)S(1)} custom-call(bf16[1024,1280]{1,0:T(8,128)(2,1)} %qi_hbm.1, bf16[1024,3456]{1,0:T(8,128)(2,1)} %qg_hbm.1, bf16[64,1280]{1,0:T(8,128)(2,1)} %fi_hbm.1, bf16[64,3456]{1,0:T(8,128)(2,1)} %fo_hbm.1, bf16[256,4096]{1,0:T(8,128)(2,1)} %store_hbm.1), custom_call_target="tpu_custom_call" | custom-call | flops 1000000000 | bytes 8000000 | tf_op jit(solution)/shard_map/pallas_call | solution.py:206
  22.3 0.7 %copy.7 = f32[256,128]{1,0:T(8,128)} copy(f32[256,128]{1,0:T(8,128)S(1)} %shard_map.55) | data formatting | bytes 262144
